TPU v7x, 32 devices: a whole 2x2x4 slice. The times are simulated.
32 devices in a mesh: vocab: 8 (over z, x), hid: 4 (over y, core).
Axes of the slice: x: 2, y: 2, z: 4, core: 2. Of those that a mesh axis runs over, the one named last changes fastest.
Arguments:
- student_hidden: bfloat16 [1024, 8192], P(None, 'hid'), as said below
- head_weight: bfloat16 [8192, 16384], P('hid', 'vocab'), as said below
- teacher_logits: bfloat16 [1024, 16384], P(('vocab', 'hid')), as said below
Outputs:
- loss_value: float32 [], replicated
- grad_hidden: bfloat16 [1024, 8192], P('vocab', 'hid')
- grad_weight: bfloat16 [8192, 16384], P('hid', 'vocab')
Inputs may be any that keep to these rules, and one draw needn't show every extreme that they name: `student_hidden`: hidden states of order one to some tens. `head_weight`: weights of order one over the square root of 8192. `teacher_logits`: logits of order one to some hundreds.
All inputs are finite; a program needn't handle non-finite values.
Results may differ from a plain program's by a relative error of at most 0.02055.
Values may be sent and summed in bfloat16 or wider, within the bound.
A program may use at most 128 MiB of HBM per device.

v0:
```python
import jax
import jax.numpy as jnp
from jax import lax
from jax.sharding import PartitionSpec as P


def row_terms(logits, teacher):
    top_student, top_teacher = lax.pmax(
        (jnp.max(logits, axis=1), jnp.max(teacher, axis=1)), "vocab"
    )
    total_student, total_teacher = lax.psum(
        (
            jnp.sum(jnp.exp(logits - top_student[:, None]), axis=1),
            jnp.sum(jnp.exp(teacher - top_teacher[:, None]), axis=1),
        ),
        "vocab",
    )
    student_log = logits - (top_student + jnp.log(total_student))[:, None]
    teacher_log = teacher - (top_teacher + jnp.log(total_teacher))[:, None]
    probs = jnp.exp(student_log)
    kl_row = lax.psum(jnp.sum(probs * (student_log - teacher_log), axis=1), "vocab")
    return (kl_row, student_log, teacher_log, probs)


def shards(student_hidden, head_weight, teacher_logits):
    n_vocab = lax.axis_size("vocab")
    tokens = student_hidden.shape[0]
    vocab_width = head_weight.shape[1]
    per_dev = teacher_logits.shape[0]
    partial_value = jnp.dot(student_hidden, head_weight, preferred_element_type=jnp.float32)
    teacher_tiles = lax.all_to_all(teacher_logits, "vocab", split_axis=1, concat_axis=0, tiled=True)
    logits = lax.psum(partial_value, "hid")
    stacked = lax.all_gather(
        teacher_tiles.reshape(n_vocab, 1, per_dev, vocab_width), "hid", axis=1, tiled=True
    )
    teacher = stacked.reshape(tokens, vocab_width).astype(jnp.float32)
    kl_row, student_log, teacher_log, probs = row_terms(logits, teacher)
    grad_logits = (probs * (student_log - teacher_log - kl_row[:, None]) / tokens).astype(
        jnp.bfloat16
    )
    loss_value = jnp.sum(kl_row) / tokens
    grad_hidden = lax.psum_scatter(
        lax.dot_general(
            grad_logits, head_weight, (((1,), (1,)), ((), ())), preferred_element_type=jnp.float32
        ).astype(jnp.bfloat16),
        "vocab",
        scatter_dimension=0,
        tiled=True,
    )
    grad_weight = lax.dot_general(
        student_hidden, grad_logits, (((0,), (0,)), ((), ())), preferred_element_type=jnp.float32
    ).astype(jnp.bfloat16)
    return (loss_value, grad_hidden, grad_weight)


def solution(mesh):
    in_specs = (P(None, "hid"), P("hid", "vocab"), P(("vocab", "hid"), None))
    out_specs = (P(), P("vocab", "hid"), P("hid", "vocab"))
    return jax.shard_map(shards, mesh=mesh, in_specs=in_specs, out_specs=out_specs, check_vma=False)
```

profile of v0, /device:TPU:8, one launch (start us, length us, event | category | flops | bytes accessed | tf_op | source)
XLA Modules:
  0.0 401.0 jit_solution(1312226934816849836)
XLA Ops:
  7.2 0.0 all-reduce.4.cloned.1.call-start
  7.2 14.5 %fusion.1 = f32[1024,2048]{1,0:T(8,128)} fusion(bf16[1024,2048]{1,0:T(8,128)(2,1)} %param.3, bf16[2048,2048]{1,0:T(8,128)(2,1)} %param.4), kind=kOutput, calls=%fused_computation.12 | convolution fusion | flops 8589934592 | bytes 20971520 | tf_op jit(solution)/shard_map/dot_general | solution.py:30
  21.7 0.0 copy-start.1
  21.7 0.0 all-reduce.4.cloned.1.call-update
  21.7 0.0 all-gather.3.cloned.1.call-start
  21.8 1.1 copy-done.1
  22.9 0.1 copy.10
  23.0 31.0 %all_to_all.16 = bf16[32,8,2048]{2,0,1:T(8,128)(2,1)} all-to-all(bf16[32,8,2048]{2,0,1:T(8,128)(2,1)S(1)} %bitcast.28), channel_id=1, replica_groups=mesh['vocab'=8,'hid'=4] {'vocab'}, dimensions={1} | all-to-all | bytes 2097152 | tf_op jit(solution)/shard_map/all_to_all | solution.py:31
  54.0 0.0 all-gather.3.cloned.1.call-update
  54.1 0.0 reduce-scatter.2.cloned.1.call-start
  54.1 121.8 %all-reduce.4.cloned.1.call-done = f32[1024,2048]{1,0:T(8,128)} async-done(((f32[1024,2048]{1,0:T(8,128)}), f32[1024,2048]{1,0:T(8,128)}) %all-reduce.4.cloned.1.call-update) | async-done | bytes 8388624 | tf_op jit(solution)/shard_map/psum | solution.py:32
  175.9 3.8 reduce_max.25
  179.7 32.4 %all-gather.3.cloned.1.call-done = bf16[8,128,2048]{2,1,0:T(8,128)(2,1)} async-done(((bf16[8,32,2048]{2,1,0:T(8,128)(2,1)}), bf16[8,128,2048]{2,1,0:T(8,128)(2,1)}) %all-gather.3.cloned.1.call-update) | async-done | bytes 4194320 | tf_op jit(solution)/shard_map/all_gather | solution.py:33
  212.1 2.8 reduce.3
  214.9 18.9 %all-reduce.1 = (f32[1024]{0:T(1024)S(1)}, f32[1024]{0:T(1024)S(1)}) all-reduce(f32[1024]{0:T(1024)S(1)} %bitcast_convert_fusion, f32[1024]{0:T(1024)S(1)} %reduce_max.25), channel_id=1, replica_groups=mesh['vocab'=8,'hid'=4] {'vocab'}, use_global_device_ids=true, to_apply=%region_6.0 | all-reduce | flops 2048 | bytes 16384 | tf_op jit(solution)/shard_map/pmax | solution.py:8
  233.8 0.1 sub.51
  233.9 3.7 exponential_reduce_fusion
  237.6 0.1 reduce_sum.40
  237.7 4.6 %exponential_reduce_fusion.1 = f32[1024]{0:T(1024)S(1)} fusion(f32[1024,2048]{1,0:T(8,128)} %all-reduce.4.cloned.1.call-done, f32[1024]{0:T(1024)S(1)} %get-tuple-element.9), kind=kLoop, calls=%fused_computation.6 | loop fusion | flops 4193280 | bytes 8396800 | tf_op jit(solution)/shard_map/reduce_sum | solution.py:13
  242.3 17.4 %all-reduce = (f32[1024]{0:T(1024)S(1)}, f32[1024]{0:T(1024)S(1)}) all-reduce(f32[1024]{0:T(1024)S(1)} %reduce_sum.40, f32[1024]{0:T(1024)S(1)} %exponential_reduce_fusion.1), channel_id=1, replica_groups=mesh['vocab'=8,'hid'=4] {'vocab'}, use_global_device_ids=true, to_apply=%region_8.0 | all-reduce | flops 2048 | bytes 16384 | tf_op jit(solution)/shard_map/psum | solution.py:11
  259.7 6.0 %multiply_reduce_fusion = f32[1024]{0:T(1024)S(1)} fusion(f32[1024,2048]{1,0:T(8,128)} %all-reduce.4.cloned.1.call-done, bf16[8,128,2048]{2,1,0:T(8,128)(2,1)} %all-gather.3.cloned.1.call-done, f32[1024]{0:T(1024)S(1)} %get-tuple-element.10, f32[1024]{0:T(1024)S(1)} %get-tuple-element.11), kind=kLoop, calls=%fused_computation.4 | loop fusion | flops 12581888 | bytes 12595200 | tf_op jit(solution)/shard_map/reduce_sum | solution.py:21
  265.7 19.3 %psum.31 = f32[1024]{0:T(1024)S(1)} all-reduce(f32[1024]{0:T(1024)S(1)} %multiply_reduce_fusion), channel_id=1, replica_groups=mesh['vocab'=8,'hid'=4] {'vocab'}, use_global_device_ids=true, to_apply=%region_10.0 | all-reduce | flops 1024 | bytes 8192 | tf_op jit(solution)/shard_map/psum | solution.py:21
  285.0 6.2 %multiply_convert_fusion = bf16[1024,2048]{1,0:T(8,128)(2,1)S(1)} fusion(f32[1024,2048]{1,0:T(8,128)} %all-reduce.4.cloned.1.call-done, bf16[8,128,2048]{2,1,0:T(8,128)(2,1)} %all-gather.3.cloned.1.call-done, f32[1024]{0:T(1024)S(1)} %psum.31, f32[1024]{0:T(1024)S(1)} %get-tuple-element.10, f32[1024]{0:T(1024)S(1)} %get-tuple-element.11), kind=kLoop, calls=%fused_computation.3 | loop fusion | flops 16777216 | bytes 16789504 | tf_op jit(solution)/shard_map/convert_element_type | solution.py:38
  291.2 0.0 copy-start
  291.3 2.0 copy-done
  293.3 12.6 %convolution_convert_fusion = bf16[1024,2048]{1,0:T(8,128)(2,1)} fusion(bf16[1024,2048]{1,0:T(8,128)(2,1)S(1)} %multiply_convert_fusion, bf16[2048,2048]{1,0:T(8,128)(2,1)} %param.4), kind=kOutput, calls=%fused_computation.7 | convolution fusion | flops 8592031744 | bytes 16777216 | tf_op jit(solution)/shard_map/dot_general | solution.py:43
  305.9 0.0 reduce-scatter.2.cloned.1.call-update
  305.9 0.6 reduce_sum.42
  306.5 14.1 %convert_bitcast_fusion = bf16[2048,2048]{0,1:T(8,128)(2,1)} fusion(bf16[1024,2048]{1,0:T(8,128)(2,1)} %copy-done, bf16[1024,2048]{1,0:T(8,128)(2,1)} %param.3), kind=kOutput, calls=%fused_computation.2 | convolution fusion | flops 8594128896 | bytes 16777216 | tf_op jit(solution)/shard_map/dot_general | solution.py:50
  320.5 12.3 %copy.7 = bf16[2048,2048]{1,0:T(8,128)(2,1)} copy(bf16[2048,2048]{0,1:T(8,128)(2,1)} %convert_bitcast_fusion) | data formatting | bytes 16777216
  333.5 59.9 %reduce-scatter.2.cloned.1.call-done = bf16[128,2048]{1,0:T(8,128)(2,1)} async-done(((bf16[1024,2048]{1,0:T(8,128)(2,1)}), bf16[128,2048]{1,0:T(8,128)(2,1)}) %reduce-scatter.2.cloned.1.call-update) | async-done | bytes 524304 | tf_op jit(solution)/shard_map/reduce_scatter | solution.py:42
  (2 shorter events, 0.0 us)
Async XLA Ops:
  7.2 168.7 %all-reduce.4.cloned.1.call-start = ((), (), s32[]{:S(2)}) async-start(), calls=%async_computation.2 | async-start | bytes 16777216 | tf_op jit(solution)/shard_map/psum | solution.py:32
  21.7 1.2 copy-start.1
  21.7 190.4 %all-gather.3.cloned.1.call-start = ((), (), s32[]{:S(2)}) async-start(), calls=%async_computation.4 | async-start | bytes 5242880 | tf_op jit(solution)/shard_map/all_gather | solution.py:33
  54.1 339.3 %reduce-scatter.2.cloned.1.call-start = ((), (), s32[]{:S(2)}) async-start(), calls=%async_computation.3 | async-start | bytes 4718592 | tf_op jit(solution)/shard_map/reduce_scatter | solution.py:42
  291.2 2.0 copy-start
Sparse Core Ops, SparseCore 0:
  21.8 154.0 all-reduce.3
  177.5 34.6 all-gather.2
  306.0 87.2 reduce-scatter.1
where the time goes:
time: 403 us; the launch traced here: 401 us
  waiting for transfers between devices  214 us (53%)
  blocking collectives  86.6 us (21%)
  matrix products  41.1 us (10%)
  other arithmetic  27.8 us (7%)
  local copies, waits for them, and re-layouts  15.7 us (4%)
  between operations  15.6 us (4%)
    psum x1, waiting for transfers between devices, shards(): logits = lax.psum(partial_value, 'hid')  122 us
    reduce_scatter x1, waiting for transfers between devices, shards(): lax.psum_scatter(lax.dot_general(grad_logits, head_weight, (((1,), (1,)),...  59.9 us
    all_gather x1, waiting for transfers between devices, shards(): lax.all_gather(teacher_tiles.reshape(n_vocab, 1, per_dev, vocab_width), '...  32.4 us
    all_to_all x1, blocking collectives, shards(): lax.all_to_all(teacher_logits, 'vocab', split_axis=1, concat_axis=0, tile...  31 us
    psum x1, blocking collectives, row_terms(): lax.psum(jnp.sum(probs * (student_log - teacher_log), axis=1), 'vocab')  19.3 us
    pmax x1, blocking collectives, row_terms(): lax.pmax((jnp.max(logits, axis=1), jnp.max(teacher, axis=1)), 'vocab')  18.9 us
    psum x1, blocking collectives, row_terms(): lax.psum((jnp.sum(jnp.exp(logits - top_student[:, None]), axis=1), jnp.su...  17.4 us
    unnamed x5, local copies, waits for them, and re-layouts  15.5 us
  transfers between devices with their start and end apart: 3, of which 3 were waited for; matrix products, arithmetic and copies ran while one was open for 8% of the time, Pallas kernels for 0%

commit v1 on v0

v1 whole, which is shorter than its diff:
```python
import jax
import jax.numpy as jnp
from jax import lax
from jax.sharding import PartitionSpec as P


def shards(student_hidden, head_weight, teacher_logits):
    n_vocab = lax.axis_size("vocab")
    n_hid = lax.axis_size("hid")
    tokens, width = student_hidden.shape
    vocab_width = head_weight.shape[1]
    per_dev = teacher_logits.shape[0]
    mine = n_vocab * per_dev
    teacher = lax.all_to_all(
        teacher_logits, "vocab", split_axis=1, concat_axis=0, tiled=True
    ).astype(jnp.float32)
    hidden = student_hidden.reshape(n_vocab, n_hid, per_dev, width)
    hidden = hidden.transpose(1, 0, 2, 3).reshape(tokens, width)
    partial_value = jnp.dot(hidden, head_weight, preferred_element_type=jnp.float32)
    logits = lax.psum_scatter(partial_value, "hid", scatter_dimension=0, tiled=True)
    top_s = jnp.max(logits, axis=1, keepdims=True)
    top_t = jnp.max(teacher, axis=1, keepdims=True)
    e = jnp.exp(logits - top_s)
    stats = jnp.stack(
        [
            top_s[:, 0],
            jnp.sum(e, axis=1),
            jnp.sum(e * ((logits - top_s) - (teacher - top_t)), axis=1),
            top_t[:, 0],
            jnp.sum(jnp.exp(teacher - top_t), axis=1),
        ]
    )
    every = lax.all_gather(stats, "vocab", axis=0)
    m_s, s_s, a, m_t, s_t = [every[:, i] for i in range(5)]
    all_s, all_t = jnp.max(m_s, axis=0), jnp.max(m_t, axis=0)
    w = jnp.exp(m_s - all_s)
    total_s = jnp.sum(w * s_s, axis=0)
    total_t = jnp.sum(jnp.exp(m_t - all_t) * s_t, axis=0)
    log_s, log_t = jnp.log(total_s), jnp.log(total_t)
    gap = (m_s - all_s) - (m_t - all_t)
    kl_row = jnp.sum(w * (a + s_s * gap), axis=0) / total_s - log_s + log_t
    loss_value = lax.psum(jnp.sum(kl_row), "hid") / tokens
    student_log = logits - (all_s + log_s)[:, None]
    teacher_log = teacher - (all_t + log_t)[:, None]
    grad = (jnp.exp(student_log) * (student_log - teacher_log - kl_row[:, None]) / tokens).astype(
        jnp.bfloat16
    )
    grad = lax.all_gather(grad, "hid", axis=0, tiled=True)
    grad_hidden = lax.dot_general(
        grad, head_weight, (((1,), (1,)), ((), ())), preferred_element_type=jnp.float32
    ).astype(jnp.bfloat16)
    grad_hidden = grad_hidden.reshape(n_hid, n_vocab, per_dev, width).transpose(1, 0, 2, 3)
    grad_hidden = lax.psum_scatter(
        grad_hidden.reshape(tokens, width), "vocab", scatter_dimension=0, tiled=True
    )
    grad_weight = lax.dot_general(
        hidden, grad, (((0,), (0,)), ((), ())), preferred_element_type=jnp.float32
    ).astype(jnp.bfloat16)
    return (loss_value, grad_hidden, grad_weight)


def solution(mesh):
    in_specs = (P(None, "hid"), P("hid", "vocab"), P(("vocab", "hid"), None))
    out_specs = (P(), P("vocab", "hid"), P("hid", "vocab"))
    return jax.shard_map(shards, mesh=mesh, in_specs=in_specs, out_specs=out_specs, check_vma=False)
```

time: 403 us -> 282 us (0.70)
  waiting for transfers between devices: 214 us -> 132 us
  blocking collectives: 86.6 us -> 65.6 us
  other arithmetic: 27.8 us -> 7.5 us
  local copies, waits for them, and re-layouts: 15.7 us -> 22.2 us
    psum x1 -> x0, waiting for transfers between devices: 122 us -> none  [shards(): logits = lax.psum(partial_value, 'hid')]
    reduce_scatter x1 -> x2, waiting for transfers between devices: 59.9 us -> 94.3 us  [the longest x1 54.5 us: shards(): lax.psum_scatter(grad_hidden.reshape(tokens, width), 'vocab', scatter_dim...]
    psum x2 -> x1, blocking collectives: 36.7 us -> 6.88 us  [shards(): loss_value = lax.psum(jnp.sum(kl_row), 'hid') / tokens]
    all_gather x0 -> x1, blocking collectives: none -> 27.8 us  [shards(): every = lax.all_gather(stats, 'vocab', axis=0)]
    pmax x1 -> x0, blocking collectives: 18.9 us -> none  [row_terms(): lax.pmax((jnp.max(logits, axis=1), jnp.max(teacher, axis=1)), 'vocab')]
    reduce_sum x4, other arithmetic: 14.9 us -> 3.49 us  [the longest x1 2.36 us: shards(): jnp.sum(e * (logits - top_s - (teacher - top_t)), axis=1)]
    transpose x0 -> x2, local copies, waits for them, and re-layouts: none -> 4.92 us  [the longest x1 2.65 us: shards(): hidden = hidden.transpose(1, 0, 2, 3).reshape(tokens, width)]
    all_gather x1, waiting for transfers between devices: 32.4 us -> 37.2 us  [shards(): grad = lax.all_gather(grad, 'hid', axis=0, tiled=True)]
  transfers between devices with their start and end apart: 3 -> 3, of which waited for: 3 -> 3; matrix products, arithmetic and copies ran while one was open for 8% -> 10% of each run, Pallas kernels for 0% -> 0%
where the time goes in v1:
time: 282 us; the launch traced here: 280 us
  waiting for transfers between devices  132 us (47%)
  blocking collectives  65.6 us (23%)
  matrix products  37.7 us (13%)
  local copies, waits for them, and re-layouts  22.2 us (8%)
  between operations  15.6 us (6%)
  other arithmetic  7.5 us (3%)
    reduce_scatter x1, waiting for transfers between devices, shards(): lax.psum_scatter(grad_hidden.reshape(tokens, width), 'vocab', scatter_dim...  54.5 us
    reduce_scatter x1, waiting for transfers between devices, shards(): lax.psum_scatter(partial_value, 'hid', scatter_dimension=0, tiled=True)  39.9 us
    all_gather x1, waiting for transfers between devices, shards(): grad = lax.all_gather(grad, 'hid', axis=0, tiled=True)  37.2 us
    all_to_all x1, blocking collectives, shards(): lax.all_to_all(teacher_logits, 'vocab', split_axis=1, concat_axis=0, tile...  30.9 us
    all_gather x1, blocking collectives, shards(): every = lax.all_gather(stats, 'vocab', axis=0)  27.8 us
    unnamed x9, local copies, waits for them, and re-layouts  16.9 us
    dot_general x1, matrix products, shards(): lax.dot_general(hidden, grad, (((0,), (0,)), ((), ())), preferred_element...  14.1 us
    dot_general x1, matrix products, shards(): lax.dot_general(grad, head_weight, (((1,), (1,)), ((), ())), preferred_el...  12.6 us
  transfers between devices with their start and end apart: 3, of which 3 were waited for; matrix products, arithmetic and copies ran while one was open for 10% of the time, Pallas kernels for 0%

profile of v1, /device:TPU:8, one launch (start us, length us, event | category | flops | bytes accessed | tf_op | source)
XLA Modules:
  0.0 280.4 jit_solution(8405380740913315697)
XLA Ops:
  7.2 0.0 reduce-scatter.3.cloned.1.call-start
  7.2 0.0 copy-start.3
  7.2 2.7 copy.28
  9.9 0.0 copy-start.1
  9.9 2.1 copy-done.1
  12.0 1.3 copy-done.3
  13.4 11.0 %fusion.17 = f32[1024,2048]{1,0:T(8,128)} fusion(bf16[1024,2048]{1,0:T(8,128)(2,1)S(1)} %bitcast.84, bf16[2048,2048]{1,0:T(8,128)(2,1)S(1)} %copy-done.3), kind=kOutput, calls=%fused_computation.36 | convolution fusion | flops 8589934592 | bytes 20971520 | tf_op jit(solution)/shard_map/dot_general | solution.py:19
  24.4 0.0 copy-start.2
  24.4 0.0 reduce-scatter.3.cloned.1.call-update
  24.4 0.0 all-gather.4.cloned.1.call-start
  24.5 1.1 copy-done.2
  25.6 0.1 copy.73
  25.7 30.9 %all_to_all.16 = bf16[32,8,2048]{2,0,1:T(8,128)(2,1)S(1)} all-to-all(bf16[32,8,2048]{2,0,1:T(8,128)(2,1)S(1)} %bitcast.87), channel_id=1, replica_groups=mesh['vocab'=8,'hid'=4] {'vocab'}, dimensions={1} | all-to-all | bytes 2097152 | tf_op jit(solution)/shard_map/all_to_all | solution.py:14
  56.6 0.2 bitcast_reduce_fusion
  56.8 0.1 reshape.81
  56.9 0.1 reshape.82
  57.0 0.5 fusion.1
  57.5 0.1 stack.14
  57.6 39.9 %reduce-scatter.3.cloned.1.call-done = f32[256,2048]{1,0:T(8,128)} async-done(((f32[1024,2048]{1,0:T(8,128)}), f32[256,2048]{1,0:T(8,128)}) %reduce-scatter.3.cloned.1.call-update) | async-done | bytes 2097168 | tf_op jit(solution)/shard_map/reduce_scatter | solution.py:20
  97.5 0.0 copy-start
  97.5 1.9 reduce_max.49
  99.4 2.4 fusion.4
  101.8 27.8 %all-gather.1 = f32[8,5,256]{2,1,0:T(8,128)S(1)} all-gather(f32[1,5,256]{2,1,0:T(8,128)S(1)} %bitcast.89), channel_id=2, replica_groups=mesh['vocab'=8,'hid'=4] {'vocab'}, dimensions={0}, use_global_device_ids=true | all-gather | bytes 46080 | tf_op jit(solution)/shard_map/all_gather | solution.py:33
  129.7 0.6 fusion.16
  130.3 0.0 copy-done
  130.3 1.8 fusion.9
  132.1 0.0 all-gather.4.cloned.1.call-update
  132.1 0.0 reduce-scatter.5.cloned.1.call-start
  132.2 37.2 %all-gather.4.cloned.1.call-done = bf16[1024,2048]{1,0:T(8,128)(2,1)} async-done(((bf16[256,2048]{1,0:T(8,128)(2,1)}), bf16[1024,2048]{1,0:T(8,128)(2,1)}) %all-gather.4.cloned.1.call-update) | async-done | bytes 4194320 | tf_op jit(solution)/shard_map/all_gather | solution.py:48
  169.4 12.6 %convolution_convert_fusion = bf16[1024,2048]{1,0:T(8,128)(2,1)S(1)} fusion(bf16[1024,2048]{1,0:T(8,128)(2,1)} %all-gather.4.cloned.1.call-done, bf16[2048,2048]{1,0:T(8,128)(2,1)} %param.4), kind=kOutput, calls=%fused_computation.1 | convolution fusion | flops 8592031744 | bytes 16777216 | tf_op jit(solution)/shard_map/dot_general | solution.py:49
  182.0 2.3 copy.34
  184.3 0.0 reduce-scatter.5.cloned.1.call-update
  184.3 6.9 %psum.7 = f32[]{:T(128)} all-reduce(f32[]{:T(128)} %get-tuple-element.22), channel_id=1, replica_groups=mesh['vocab'=8,'hid'=4] {'hid'}, use_global_device_ids=true, to_apply=%region_12.0 | all-reduce | flops 1 | bytes 8 | tf_op jit(solution)/shard_map/psum | solution.py:42
  191.8 14.1 %convert_bitcast_fusion = bf16[2048,2048]{0,1:T(8,128)(2,1)} fusion(bf16[1024,2048]{1,0:T(8,128)(2,1)} %all-gather.4.cloned.1.call-done, bf16[1024,2048]{1,0:T(8,128)(2,1)} %bitcast.85), kind=kOutput, calls=%fused_computation | convolution fusion | flops 8594128896 | bytes 16777216 | tf_op jit(solution)/shard_map/dot_general | solution.py:56
  205.9 12.3 %copy.35 = bf16[2048,2048]{1,0:T(8,128)(2,1)} copy(bf16[2048,2048]{0,1:T(8,128)(2,1)} %convert_bitcast_fusion) | data formatting | bytes 16777216
  218.2 54.5 %reduce-scatter.5.cloned.1.call-done = bf16[128,2048]{1,0:T(8,128)(2,1)} async-done(((bf16[1024,2048]{1,0:T(8,128)(2,1)}), bf16[128,2048]{1,0:T(8,128)(2,1)}) %reduce-scatter.5.cloned.1.call-update) | async-done | bytes 524304 | tf_op jit(solution)/shard_map/reduce_scatter | solution.py:53
  (4 shorter events, 0.1 us)
Async XLA Ops:
  7.2 90.3 %reduce-scatter.3.cloned.1.call-start = ((), (), s32[]{:S(2)}) async-start(), calls=%async_computation.3 | async-start | bytes 10485760 | tf_op jit(solution)/shard_map/reduce_scatter | solution.py:20
  7.2 6.2 %copy-start.3 = (bf16[2048,2048]{1,0:T(8,128)(2,1)S(1)}, bf16[2048,2048]{1,0:T(8,128)(2,1)}, u32[]{:S(2)}) copy-start(bf16[2048,2048]{1,0:T(8,128)(2,1)} %param.4) | copy-start | bytes 25165828
  9.9 2.1 copy-start.1
  24.4 1.2 copy-start.2
  24.4 145.0 %all-gather.4.cloned.1.call-start = ((), (), s32[]{:S(2)}) async-start(), calls=%async_computation.4 | async-start | bytes 5242880 | tf_op jit(solution)/shard_map/all_gather | solution.py:48
  97.5 32.8 %copy-start = (f32[256,2048]{1,0:T(8,128)S(1)}, f32[256,2048]{1,0:T(8,128)}, u32[]{:S(2)}) copy-start(f32[256,2048]{1,0:T(8,128)} %reduce-scatter.3.cloned.1.call-done) | copy-start | bytes 6291460
  132.1 140.6 %reduce-scatter.5.cloned.1.call-start = ((), (), s32[]{:S(2)}) async-start(), calls=%async_computation.5 | async-start | bytes 4718592 | tf_op jit(solution)/shard_map/reduce_scatter | solution.py:53
Sparse Core Ops, SparseCore 0:
  24.5 72.8 reduce-scatter.2
  132.3 37.1 all-gather.3
  184.4 88.2 reduce-scatter.4

commit v2 on v1

--- a/solution.py
+++ b/solution.py
@@ -1,7 +1,371 @@
+import functools
+
 import jax
 import jax.numpy as jnp
 from jax import lax
+from jax.experimental import pallas as pl
+from jax.experimental.pallas import tpu as pltpu
 from jax.sharding import PartitionSpec as P
+
+
+F32, BF16 = jnp.float32, jnp.bfloat16
+HI, LO = 4095.0, 2047.0
+
+
+def fused(
+    tokens, hid, wgt, teach, loss_o, gh_o, gw_o,
+    W, H, T, SC, RC, SY, RY, XF, LG, STS, STR, TB, KLS, KLR, G, RT, GHS, GHR, GHK, ZS, ZR, GWS,
+    ld, t_s, t_r, c_s, c_r, y_s, y_r, st_s, st_r, g_s, g_r, kl_s, kl_r, x_s, x_r, z_s, z_r, gw_s,
+):
+    nv, nh, per, width = hid.shape
+    vw = wgt.shape[1]
+    half = per // 2
+    rows = nv * half
+    nz, ncb = nv // 2, GHS.shape[0] // 2
+    cw = width // ncb
+    nt = vw // 4
+    hv = vw // 2
+    me_v, me_h = lax.axis_index("vocab"), lax.axis_index("hid")
+    y, c = me_h // 2, me_h % 2
+    z, x = me_v // 2, me_v % 2
+    h_core, h_y, h_far = 2 * y + 1 - c, 2 * (1 - y) + c, 2 * (1 - y) + 1 - c
+
+    def remote(src, dst, send, recv, v, h):
+        return pltpu.make_async_remote_copy(
+            src_ref=src, dst_ref=dst, send_sem=send, recv_sem=recv,
+            device_id={"vocab": v, "hid": h}, device_id_type=pl.DeviceIdType.MESH,
+        )
+
+    loads = [
+        pltpu.make_async_copy(hid.at[:, h, pl.ds(th * half, half), :], H.at[h, th], ld.at[2 * h + th])
+        for h in range(nh) for th in range(2)
+    ]
+    loads.append(pltpu.make_async_copy(wgt, W, ld.at[2 * nh]))
+    for copy in loads:
+        copy.start()
+
+    def teach_part(th, v):
+        return teach.at[pl.ds(th * half, half), pl.ds(pl.multiple_of(v * vw, vw), vw)]
+
+    own_t = [
+        pltpu.make_async_copy(teach_part(th, me_v), T.at[th, me_v], ld.at[2 * nh + 1 + th]) for th in range(2)
+    ]
+    for copy in own_t:
+        copy.start()
+
+    barrier = pltpu.get_barrier_semaphore()
+    for h in (h_core, h_y, h_far):
+        pl.semaphore_signal(
+            barrier, inc=1, device_id={"vocab": me_v, "hid": h}, device_id_type=pl.DeviceIdType.MESH
+        )
+    for k in range(1, nv):
+        pl.semaphore_signal(
+            barrier, inc=1, device_id={"vocab": (me_v + k) % nv, "hid": me_h},
+            device_id_type=pl.DeviceIdType.MESH,
+        )
+    pl.semaphore_wait(barrier, nh - 1 + nv - 1)
+
+    def send_t(th, k):
+        v = (me_v + k) % nv
+        return remote(teach_part(th, v), T.at[th, me_v], t_s.at[th, k], t_r.at[th, k], v, me_h)
+
+    for th in range(2):
+        for k in range(1, nv):
+            send_t(th, k).start()
+    for copy in loads:
+        copy.wait()
+
+    def project(h, out):
+        @pl.loop(0, vw // nt)
+        def _(i):
+            cols = pl.ds(pl.multiple_of(i * nt, nt), nt)
+            r = jnp.dot(H[h].reshape(2 * rows, width), W[:, cols], preferred_element_type=F32)
+            out[:, :, cols] = r.reshape(2, rows, nt)
+
+    def core_copy(kind, th):
+        return remote(
+            SC.at[kind, th], RC.at[kind, th], c_s.at[kind, th], c_r.at[kind, th], me_v, h_core
+        )
+
+    def y_copy(th):
+        return remote(SY.at[th], RY.at[th], y_s.at[th], y_r.at[th], me_v, h_y)
+
+    project(h_far, SC.at[0])
+    for th in range(2):
+        core_copy(0, th).start()
+    project(h_y, XF)
+    for th in range(2):
+        core_copy(0, th).wait_recv()
+
+        @pl.loop(0, nv)
+        def _(i):
+            r16 = pl.ds(pl.multiple_of(i * half, half), half)
+            s = XF[th, r16] + RC[0, th, r16]
+            top = jnp.maximum(jnp.max(jnp.abs(s), axis=1, keepdims=True), 1e-20)
+            hi = jnp.floor(s[:, :hv] * (HI / top) + 0.5)
+            lo = jnp.floor(s[:, hv:] * (LO / top) + 0.5)
+            SY[th, r16, pl.ds(0, hv)] = hi * 4096.0 + lo
+            SY[th, r16, pl.ds(hv, 128)] = jnp.broadcast_to(top, (half, 128))
+
+        y_copy(th).start()
+    project(h_core, SC.at[1])
+    for th in range(2):
+        core_copy(1, th).start()
+    project(me_h, LG)
+
+    lane = lax.broadcasted_iota(jnp.int32, (half, rows), 1)
+    KLS[...] = jnp.zeros_like(KLS)
+
+    def st_copy(th, k):
+        return remote(
+            STS.at[th], STR.at[th, me_v], st_s.at[th, k], st_r.at[th, k], (me_v + k) % nv, me_h
+        )
+
+    def stats(th):
+        core_copy(1, th).wait_recv()
+        y_copy(th).wait_recv()
+        own_t[th].wait()
+        for k in range(1, nv):
+            send_t(th, k).wait_recv()
+
+        @pl.loop(0, nv)
+        def _(i):
+            r16 = pl.ds(pl.multiple_of(i * half, half), half)
+            f = RY[th, r16, pl.ds(0, hv)]
+            top = RY[th, r16, pl.ds(hv, 128)][:, 0:1]
+            hi = jnp.floor(f * (1.0 / 4096.0) + 0.5)
+            lo = f - hi * 4096.0
+            both = jnp.concatenate([hi * (top / HI), lo * (top / LO)], axis=1)
+            l = LG[th, r16] + RC[1, th, r16] + both
+            LG[th, r16] = l
+            t = T[th, i].astype(F32)
+            m = jnp.max(l, axis=1, keepdims=True)
+            mt = jnp.max(t, axis=1, keepdims=True)
+            l, t = l - m, t - mt
+            e = jnp.exp(l)
+            cols = [
+                m, jnp.sum(e, axis=1, keepdims=True), jnp.sum(e * (l - t), axis=1, keepdims=True),
+                mt, jnp.sum(jnp.exp(t), axis=1, keepdims=True),
+            ]
+            block = jnp.zeros((half, rows), F32)
+            for j, col in enumerate(cols):
+                block = jnp.where(lane == j, col, block)
+            TB[r16, :] = block
+
+        flat = TB[...].T[0:8]
+        STS[th] = flat
+        STR[th, me_v] = flat
+        for k in range(1, nv):
+            st_copy(th, k).start()
+
+    def g_copy(th, which):
+        if which == 0:
+            return remote(G.at[me_h, th], G.at[me_h, th], g_s.at[th, 0], g_r.at[th, 0], me_v, h_core)
+        if which == 1:
+            return remote(G.at[me_h, th], G.at[me_h, th], g_s.at[th, 1], g_r.at[th, 1], me_v, h_y)
+        return remote(G.at[h_y, th], G.at[h_y, th], g_s.at[th, 2], g_r.at[th, 2], me_v, h_core)
+
+    def grad(th):
+        for k in range(1, nv):
+            st_copy(th, k).wait_recv()
+        p = [STR[th, d] for d in range(nv)]
+        m_s, s_s, a, m_t, s_t = [[q[j : j + 1] for q in p] for j in range(5)]
+        top_s, top_t = functools.reduce(jnp.maximum, m_s), functools.reduce(jnp.maximum, m_t)
+        total_s = total_t = total_a = jnp.zeros_like(top_s)
+        for d in range(nv):
+            w = jnp.exp(m_s[d] - top_s)
+            total_s = total_s + w * s_s[d]
+            total_t = total_t + jnp.exp(m_t[d] - top_t) * s_t[d]
+            total_a = total_a + w * (a[d] + s_s[d] * ((m_s[d] - top_s) - (m_t[d] - top_t)))
+        log_s, log_t = jnp.log(total_s), jnp.log(total_t)
+        kl = total_a / total_s - log_s + log_t
+        KLS[th : th + 1, :] = kl
+        TB[0:1, :] = top_s + log_s
+        TB[1:2, :] = top_t + log_t
+        TB[2:3, :] = kl
+        TB[...] = TB[...].T
+
+        @pl.loop(0, nv)
+        def _(i):
+            r16 = pl.ds(pl.multiple_of(i * half, half), half)
+            b = TB[r16, :]
+            u = LG[th, r16] - b[:, 0:1]
+            gap = u - (T[th, i].astype(F32) - b[:, 1:2])
+            G[me_h, th, r16] = (jnp.exp(u) * (gap - b[:, 2:3]) / tokens).astype(BF16)
+
+        g_copy(th, 1).start()
+        g_copy(th, 0).start()
+
+    def kl_copy(k):
+        return remote(KLS, KLR.at[me_h], kl_s.at[k], kl_r.at[k], me_v, (me_h + k) % nh)
+
+    stats(0)
+    grad(0)
+    stats(1)
+    grad(1)
+    KLR[me_h] = KLS[...]
+    for k in range(1, nh):
+        kl_copy(k).start()
+
+    def x_copy(s):
+        return remote(GHS.at[s], GHR.at[s], x_s.at[s], x_r.at[s], 2 * z + 1 - x, me_h)
+
+    def z_copy(s, k):
+        to = (z + k) % nz
+        return remote(ZS.at[s, to], ZR.at[s, z], z_s.at[s, k], z_r.at[s, k], 2 * to + x, me_h)
+
+    def hidden_part(th):
+        g_copy(th, 1).wait_recv()
+        g_copy(th, 2).start()
+        g_copy(th, 0).wait_recv()
+        g_copy(th, 2).wait_recv()
+
+        @pl.loop(0, ncb)
+        def _(cb):
+            s = th * ncb + cb
+            r = lax.dot_general(
+                G[:, th].reshape(nh * rows, vw), W[pl.ds(pl.multiple_of(cb * cw, cw), cw), :],
+                (((1,), (1,)), ((), ())), preferred_element_type=F32,
+            )
+            RT[...] = r.reshape(nh, nz, 2, half, cw)
+            GHS[s] = RT[:, :, 1 - x].astype(BF16)
+            x_copy(s).start()
+            GHK[s] = RT[:, :, x]
+
+    def pass_on(s):
+        x_copy(s).wait_recv()
+        for to in range(nz):
+            ZS[s, to] = (GHK[s, :, to] + GHR[s, :, to].astype(F32)).astype(BF16)
+        for k in range(1, nz):
+            z_copy(s, k).start()
+
+    tile = width // 8
+
+    def gw_copy(i, slot):
+        return pltpu.make_async_copy(
+            GWS.at[slot], gw_o.at[pl.ds(pl.multiple_of(i * tile, tile), tile), :], gw_s.at[slot]
+        )
+
+    def weight_tile(i):
+        slot = i % 2
+
+        @pl.when(i >= 2)
+        def _():
+            gw_copy(i - 2, slot).wait()
+
+        h = H[:, :, :, :, pl.ds(pl.multiple_of(i * tile, tile), tile)].reshape(2 * nh * rows, tile)
+
+        @pl.loop(0, vw // nt)
+        def _(j):
+            cols = pl.ds(pl.multiple_of(j * nt, nt), nt)
+            GWS[slot, :, cols] = lax.dot_general(
+                h, G[:, :, :, cols].reshape(2 * nh * rows, nt),
+                (((0,), (0,)), ((), ())), preferred_element_type=F32,
+            ).astype(BF16)
+
+        gw_copy(i, slot).start()
+
+    hidden_part(0)
+    pass_on(0)
+    pass_on(1)
+    hidden_part(1)
+
+    @pl.loop(0, 8)
+    def _(i):
+        weight_tile(i)
+
+        @pl.when(i < 2 * ncb - 2)
+        def _():
+            pass_on(i + 2)
+
+    for i in (6, 7):
+        gw_copy(i, i % 2).wait()
+    for th in range(2):
+        @pl.loop(0, ncb)
+        def _(cb):
+            s = th * ncb + cb
+            total = ZS[s, z].astype(F32)
+            for k in range(1, nz):
+                z_copy(s, k).wait_recv()
+                total = total + ZR[s, (z + nz - k) % nz].astype(F32)
+            cols = pl.ds(pl.multiple_of(cb * cw, cw), cw)
+            gh_o[:, pl.ds(th * half, half), cols] = total.astype(BF16)
+            x_copy(s).wait_send()
+            for k in range(1, nz):
+                z_copy(s, k).wait_send()
+
+    for k in range(1, nh):
+        kl_copy(k).wait()
+    kl_all = functools.reduce(jnp.add, [KLR[h] for h in range(nh)])
+    kl_all = jnp.sum(jnp.sum(kl_all, axis=1, keepdims=True), axis=0, keepdims=True) / tokens
+    loss_o[...] = jnp.broadcast_to(kl_all, loss_o.shape)
+    for th in range(2):
+        y_copy(th).wait_send()
+        for kind in range(2):
+            core_copy(kind, th).wait_send()
+        for which in range(3):
+            g_copy(th, which).wait_send()
+        for k in range(1, nv):
+            send_t(th, k).wait_send()
+            st_copy(th, k).wait_send()
+
+
+def fused_shards(student_hidden, head_weight, teacher_logits):
+    nv, nh = lax.axis_size("vocab"), lax.axis_size("hid")
+    tokens, width = student_hidden.shape
+    vw = head_weight.shape[1]
+    per = teacher_logits.shape[0]
+    half, nz, ncb = per // 2, nv // 2, 4
+    rows, cw, tile = nv * half, width // ncb, width // 8
+    hidden = student_hidden.reshape(nv, nh, per, width)
+    any_, vmem = pl.BlockSpec(memory_space=pl.ANY), pl.BlockSpec(memory_space=pltpu.VMEM)
+    dma = lambda *shape: pltpu.SemaphoreType.DMA(shape)
+    steps = 2 * ncb
+    loss, gh, gw = pl.pallas_call(
+        functools.partial(fused, tokens),
+        out_shape=(
+            jax.ShapeDtypeStruct((8, 128), F32),
+            jax.ShapeDtypeStruct((nh, per, width), BF16),
+            jax.ShapeDtypeStruct((width, vw), BF16),
+        ),
+        in_specs=[any_, any_, any_],
+        out_specs=(vmem, vmem, any_),
+        scratch_shapes=[
+            pltpu.VMEM((width, vw), BF16),
+            pltpu.VMEM((nh, 2, nv, half, width), BF16),
+            pltpu.VMEM((2, nv, half, vw), BF16),
+            pltpu.VMEM((2, 2, rows, vw), F32),
+            pltpu.VMEM((2, 2, rows, vw), F32),
+            pltpu.VMEM((2, rows, vw // 2 + 128), F32),
+            pltpu.VMEM((2, rows, vw // 2 + 128), F32),
+            pltpu.VMEM((2, rows, vw), F32),
+            pltpu.VMEM((2, rows, vw), F32),
+            pltpu.VMEM((2, 8, rows), F32),
+            pltpu.VMEM((2, nv, 8, rows), F32),
+            pltpu.VMEM((rows, rows), F32),
+            pltpu.VMEM((8, rows), F32),
+            pltpu.VMEM((nh, 8, rows), F32),
+            pltpu.VMEM((nh, 2, rows, vw), BF16),
+            pltpu.VMEM((nh, nz, 2, half, cw), F32),
+            pltpu.VMEM((steps, nh, nz, half, cw), BF16),
+            pltpu.VMEM((steps, nh, nz, half, cw), BF16),
+            pltpu.VMEM((steps, nh, nz, half, cw), F32),
+            pltpu.VMEM((steps, nz, nh, half, cw), BF16),
+            pltpu.VMEM((steps, nz, nh, half, cw), BF16),
+            pltpu.VMEM((2, tile, vw), BF16),
+            dma(2 * nh + 3),
+            dma(2, nv), dma(2, nv), dma(2, 2), dma(2, 2), dma(2), dma(2), dma(2, nv), dma(2, nv),
+            dma(2, 3), dma(2, 3), dma(nh), dma(nh), dma(steps), dma(steps), dma(steps, nz), dma(steps, nz),
+            dma(2),
+        ],
+        compiler_params=pltpu.CompilerParams(
+            collective_id=0, has_side_effects=True, vmem_limit_bytes=60 * 1024 * 1024
+        ),
+        cost_estimate=pl.CostEstimate(
+            flops=6 * tokens * width * vw, bytes_accessed=4 * width * vw, transcendentals=0
+        ),
+    )(hidden, head_weight, teacher_logits)
+    return loss[0, 0], gh.reshape(nh * per, width), gw
 
 
 def shards(student_hidden, head_weight, teacher_logits):
@@ -60,6 +424,11 @@
 
 
 def solution(mesh):
+    fits = mesh.shape["hid"] == 4 and mesh.shape["vocab"] == 8
+    def body(student_hidden, head_weight, teacher_logits):
+        ok = fits and teacher_logits.shape[0] == 32
+        return (fused_shards if ok else shards)(student_hidden, head_weight, teacher_logits)
+
     in_specs = (P(None, "hid"), P("hid", "vocab"), P(("vocab", "hid"), None))
     out_specs = (P(), P("vocab", "hid"), P("hid", "vocab"))
-    return jax.shard_map(shards, mesh=mesh, in_specs=in_specs, out_specs=out_specs, check_vma=False)
+    return jax.shard_map(body, mesh=mesh, in_specs=in_specs, out_specs=out_specs, check_vma=False)

time: 282 us -> 128 us (0.45)
  waiting for transfers between devices: 132 us -> 0 us
  Pallas kernels: 0 us -> 114 us
  blocking collectives: 65.6 us -> 0 us
  matrix products: 37.7 us -> 0 us
  between operations: 15.6 us -> 0.64 us
  local copies, waits for them, and re-layouts: 22.2 us -> 11.5 us
  other arithmetic: 7.5 us -> 0 us
    pallas_call x0 -> x1, Pallas kernels: none -> 114 us  [fused_shards(): pl.pallas_call(functools.partial(fused, tokens), out_shape=(jax.ShapeDtyp...]
    reduce_scatter x2 -> x0, waiting for transfers between devices: 94.3 us -> none  [the longest x1 54.5 us: shards(): lax.psum_scatter(grad_hidden.reshape(tokens, width), 'vocab', scatter_dim...]
    dot_general x3 -> x0, matrix products: 37.7 us -> none  [the longest x1 14.1 us: shards(): lax.dot_general(hidden, grad, (((0,), (0,)), ((), ())), preferred_element...]
    all_gather x1 -> x0, waiting for transfers between devices: 37.2 us -> none  [shards(): grad = lax.all_gather(grad, 'hid', axis=0, tiled=True)]
    all_to_all x1 -> x0, blocking collectives: 30.9 us -> none  [shards(): lax.all_to_all(teacher_logits, 'vocab', split_axis=1, concat_axis=0, tile...]
    all_gather x1 -> x0, blocking collectives: 27.8 us -> none  [shards(): every = lax.all_gather(stats, 'vocab', axis=0)]
    psum x1 -> x0, blocking collectives: 6.88 us -> none  [shards(): loss_value = lax.psum(jnp.sum(kl_row), 'hid') / tokens]
    unnamed x9 -> x2, local copies, waits for them, and re-layouts: 16.9 us -> 10.3 us
  transfers between devices with their start and end apart: 3 -> 0, of which waited for: 3 -> 0; matrix products, arithmetic and copies ran while one was open for 10% -> 0% of each run, Pallas kernels for 0% -> 0%
where the time goes in v2:
time: 128 us; the launch traced here: 126 us
  Pallas kernels  114 us (89%)
  local copies, waits for them, and re-layouts  11.5 us (9%)
    pallas_call x1, Pallas kernels, fused_shards(): pl.pallas_call(functools.partial(fused, tokens), out_shape=(jax.ShapeDtyp...  114 us
    unnamed x2, local copies, waits for them, and re-layouts  10.3 us

profile of v2, /device:TPU:8, one launch (start us, length us, event | category | flops | bytes accessed | tf_op | source)
XLA Modules:
  0.0 126.3 jit_solution(1968243193638636164)
XLA Ops:
  0.6 114.2 %shard_map.58 = (f32[8,128]{1,0:T(8,128)}, bf16[4,32,2048]{2,1,0:T(8,128)(2,1)}, bf16[2048,2048]{1,0:T(8,128)(2,1)}) custom-call(bf16[8,4,32,2048]{3,2,1,0:T(8,128)(2,1)} %bitcast.4, bf16[2048,2048]{1,0:T(8,128)(2,1)} %wgt.1, bf16[32,16384]{1,0:T(8,128)(2,1)} %teach.1), custom_call_target="tpu_custom_call" | custom-call | flops 25769803776 | bytes 16777216 | tf_op jit(solution)/shard_map/pallas_call | solution.py:324
  114.8 1.2 slice.3
  116.0 1.9 %copy.8 = bf16[128,2048]{1,0:T(8,128)(2,1)} copy(bf16[128,2048]{1,0:T(8,128)(2,1)} %bitcast.3) | data formatting | bytes 1048576
  117.9 8.4 %copy.9 = bf16[2048,2048]{1,0:T(8,128)(2,1)} copy(bf16[2048,2048]{1,0:T(8,128)(2,1)} %get-tuple-element.14) | data formatting | bytes 16777216

commit v3 on v2

--- a/solution.py
+++ b/solution.py
@@ -36,19 +36,28 @@
             device_id={"vocab": v, "hid": h}, device_id_type=pl.DeviceIdType.MESH,
         )
 
-    loads = [
-        pltpu.make_async_copy(hid.at[:, h, pl.ds(th * half, half), :], H.at[h, th], ld.at[2 * h + th])
-        for h in range(nh) for th in range(2)
-    ]
-    loads.append(pltpu.make_async_copy(wgt, W, ld.at[2 * nh]))
-    for copy in loads:
-        copy.start()
+    def load_h(k, th):
+        h = (h_far, h_y, h_core, me_h)[k]
+        return pltpu.make_async_copy(
+            hid.at[:, h, pl.ds(th * half, half), :], H.at[h, th], ld.at[2 * k + th]
+        )
+
+    def load_w(i):
+        cols = pl.ds(pl.multiple_of(i * nt, nt), nt)
+        return pltpu.make_async_copy(wgt.at[:, cols], W.at[:, cols], ld.at[2 * nh + 2 + i])
+
+    for k in range(nh):
+        for th in range(2):
+            load_h(k, th).start()
+        if k == 0:
+            for i in range(vw // nt):
+                load_w(i).start()
 
     def teach_part(th, v):
         return teach.at[pl.ds(th * half, half), pl.ds(pl.multiple_of(v * vw, vw), vw)]
 
     own_t = [
-        pltpu.make_async_copy(teach_part(th, me_v), T.at[th, me_v], ld.at[2 * nh + 1 + th]) for th in range(2)
+        pltpu.make_async_copy(teach_part(th, me_v), T.at[th, me_v], ld.at[2 * nh + th]) for th in range(2)
     ]
     for copy in own_t:
         copy.start()
@@ -69,15 +78,18 @@
         v = (me_v + k) % nv
         return remote(teach_part(th, v), T.at[th, me_v], t_s.at[th, k], t_r.at[th, k], v, me_h)
 
-    for th in range(2):
-        for k in range(1, nv):
-            send_t(th, k).start()
-    for copy in loads:
-        copy.wait()
-
-    def project(h, out):
+    for k in range(1, nv):
+        send_t(0, k).start()
+
+    def project(k, out):
+        h = (h_far, h_y, h_core, me_h)[k]
+        for th in range(2):
+            load_h(k, th).wait()
+
         @pl.loop(0, vw // nt)
         def _(i):
+            if k == 0:
+                load_w(i).wait()
             cols = pl.ds(pl.multiple_of(i * nt, nt), nt)
             r = jnp.dot(H[h].reshape(2 * rows, width), W[:, cols], preferred_element_type=F32)
             out[:, :, cols] = r.reshape(2, rows, nt)
@@ -90,10 +102,10 @@
     def y_copy(th):
         return remote(SY.at[th], RY.at[th], y_s.at[th], y_r.at[th], me_v, h_y)
 
-    project(h_far, SC.at[0])
+    project(0, SC.at[0])
     for th in range(2):
         core_copy(0, th).start()
-    project(h_y, XF)
+    project(1, XF)
     for th in range(2):
         core_copy(0, th).wait_recv()
 
@@ -107,11 +119,14 @@
             SY[th, r16, pl.ds(0, hv)] = hi * 4096.0 + lo
             SY[th, r16, pl.ds(hv, 128)] = jnp.broadcast_to(top, (half, 128))
 
-        y_copy(th).start()
-    project(h_core, SC.at[1])
+        if th == 0:
+            y_copy(0).start()
+    project(2, SC.at[1])
     for th in range(2):
         core_copy(1, th).start()
-    project(me_h, LG)
+    project(3, LG)
+    for k in range(1, nv):
+        send_t(1, k).start()
 
     lane = lax.broadcasted_iota(jnp.int32, (half, rows), 1)
     KLS[...] = jnp.zeros_like(KLS)
@@ -124,6 +139,9 @@
     def stats(th):
         core_copy(1, th).wait_recv()
         y_copy(th).wait_recv()
+        if th == 0:
+            y_copy(0).wait_send()
+            y_copy(1).start()
         own_t[th].wait()
         for k in range(1, nv):
             send_t(th, k).wait_recv()
@@ -229,11 +247,19 @@
             )
             RT[...] = r.reshape(nh, nz, 2, half, cw)
             GHS[s] = RT[:, :, 1 - x].astype(BF16)
-            x_copy(s).start()
+            if th == 0:
+                @pl.when(cb < 2)
+                def _():
+                    x_copy(s).start()
             GHK[s] = RT[:, :, x]
 
     def pass_on(s):
-        x_copy(s).wait_recv()
+        x_copy(s).wait()
+
+        @pl.when(s < 2 * ncb - 2)
+        def _():
+            x_copy(s + 2).start()
+
         for to in range(nz):
             ZS[s, to] = (GHK[s, :, to] + GHR[s, :, to].astype(F32)).astype(BF16)
         for k in range(1, nz):
@@ -290,7 +316,6 @@
                 total = total + ZR[s, (z + nz - k) % nz].astype(F32)
             cols = pl.ds(pl.multiple_of(cb * cw, cw), cw)
             gh_o[:, pl.ds(th * half, half), cols] = total.astype(BF16)
-            x_copy(s).wait_send()
             for k in range(1, nz):
                 z_copy(s, k).wait_send()
 
@@ -298,9 +323,9 @@
         kl_copy(k).wait()
     kl_all = functools.reduce(jnp.add, [KLR[h] for h in range(nh)])
     kl_all = jnp.sum(jnp.sum(kl_all, axis=1, keepdims=True), axis=0, keepdims=True) / tokens
-    loss_o[...] = jnp.broadcast_to(kl_all, loss_o.shape)
+    loss_o[...] = kl_all
+    y_copy(1).wait_send()
     for th in range(2):
-        y_copy(th).wait_send()
         for kind in range(2):
             core_copy(kind, th).wait_send()
         for which in range(3):
@@ -308,6 +333,23 @@
         for k in range(1, nv):
             send_t(th, k).wait_send()
             st_copy(th, k).wait_send()
+
+
+def hand_out(loss, gh, gw, loss_o, gh_o, gw_o, buf, buf_h, sem_in, sem_out):
+    part = gw.shape[0] // 8
+    blocks = [pl.ds(i * part, part) for i in range(8)]
+    read = [pltpu.make_async_copy(gw.at[b], buf.at[b], sem_in.at[i]) for i, b in enumerate(blocks)]
+    write = [pltpu.make_async_copy(buf.at[b], gw_o.at[b], sem_out.at[i]) for i, b in enumerate(blocks)]
+    read.append(pltpu.make_async_copy(gh, buf_h, sem_in.at[8]))
+    write.append(pltpu.make_async_copy(buf_h, gh_o, sem_out.at[8]))
+    for copy in read:
+        copy.start()
+    loss_o[...] = loss[...]
+    for copy, after in zip(read, write):
+        copy.wait()
+        after.start()
+    for copy in write:
+        copy.wait()
 
 
 def fused_shards(student_hidden, head_weight, teacher_logits):
@@ -324,7 +366,7 @@
     loss, gh, gw = pl.pallas_call(
         functools.partial(fused, tokens),
         out_shape=(
-            jax.ShapeDtypeStruct((8, 128), F32),
+            jax.ShapeDtypeStruct((1, 1), F32),
             jax.ShapeDtypeStruct((nh, per, width), BF16),
             jax.ShapeDtypeStruct((width, vw), BF16),
         ),
@@ -353,7 +395,7 @@
             pltpu.VMEM((steps, nz, nh, half, cw), BF16),
             pltpu.VMEM((steps, nz, nh, half, cw), BF16),
             pltpu.VMEM((2, tile, vw), BF16),
-            dma(2 * nh + 3),
+            dma(2 * nh + 2 + 4),
             dma(2, nv), dma(2, nv), dma(2, 2), dma(2, 2), dma(2), dma(2), dma(2, nv), dma(2, nv),
             dma(2, 3), dma(2, 3), dma(nh), dma(nh), dma(steps), dma(steps), dma(steps, nz), dma(steps, nz),
             dma(2),
@@ -365,7 +407,16 @@
             flops=6 * tokens * width * vw, bytes_accessed=4 * width * vw, transcendentals=0
         ),
     )(hidden, head_weight, teacher_logits)
-    return loss[0, 0], gh.reshape(nh * per, width), gw
+    loss, gh, gw = pl.pallas_call(
+        hand_out,
+        out_shape=tuple(jax.ShapeDtypeStruct(a.shape, a.dtype) for a in (loss, gh, gw)),
+        in_specs=[vmem, any_, any_],
+        out_specs=(vmem, any_, any_),
+        scratch_shapes=[pltpu.VMEM(gw.shape, BF16), pltpu.VMEM(gh.shape, BF16), dma(9), dma(9)],
+        compiler_params=pltpu.CompilerParams(vmem_limit_bytes=60 * 1024 * 1024),
+        cost_estimate=pl.CostEstimate(flops=0, bytes_accessed=4 * width * vw, transcendentals=0),
+    )(loss, gh, gw)
+    return loss.reshape(()), gh.reshape(nh * per, width), gw
 
 
 def shards(student_hidden, head_weight, teacher_logits):

time: 128 us -> 123 us (0.961)
  local copies, waits for them, and re-layouts: 11.5 us -> 0 us
  Pallas kernels: 114 us -> 121 us
    unnamed x2 -> x0, local copies, waits for them, and re-layouts: 10.3 us -> none
    pallas_call x0 -> x1, Pallas kernels: none -> 7.69 us  [fused_shards(): pl.pallas_call(hand_out, out_shape=tuple((jax.ShapeDtypeStruct(a.shape, a...]
where the time goes in v3:
time: 123 us; the launch traced here: 121 us
  Pallas kernels  121 us (98%)
    pallas_call x1, Pallas kernels, fused_shards(): pl.pallas_call(functools.partial(fused, tokens), out_shape=(jax.ShapeDtyp...  113 us
    pallas_call x1, Pallas kernels, fused_shards(): pl.pallas_call(hand_out, out_shape=tuple((jax.ShapeDtypeStruct(a.shape, a...  7.69 us

profile of v3, /device:TPU:8, one launch (start us, length us, event | category | flops | bytes accessed | tf_op | source)
XLA Modules:
  0.0 121.3 jit_solution(14115009377499776417)
XLA Ops:
  0.6 112.9 %shard_map.58 = (f32[1,1]{1,0:T(1,128)}, bf16[4,32,2048]{2,1,0:T(8,128)(2,1)}, bf16[2048,2048]{1,0:T(8,128)(2,1)}) custom-call(bf16[8,4,32,2048]{3,2,1,0:T(8,128)(2,1)} %bitcast.3, bf16[2048,2048]{1,0:T(8,128)(2,1)} %wgt.1, bf16[32,16384]{1,0:T(8,128)(2,1)} %teach.1), custom_call_target="tpu_custom_call" | custom-call | flops 25769803776 | bytes 16777216 | tf_op jit(solution)/shard_map/pallas_call | solution.py:366
  113.6 7.7 %shard_map.59 = (f32[1,1]{1,0:T(1,128)}, bf16[4,32,2048]{2,1,0:T(8,128)(2,1)}, bf16[2048,2048]{1,0:T(8,128)(2,1)}) custom-call(f32[1,1]{1,0:T(1,128)} %get-tuple-element.9.loss, bf16[4,32,2048]{2,1,0:T(8,128)(2,1)} %get-tuple-element.10.gh, bf16[2048,2048]{1,0:T(8,128)(2,1)} %get-tuple-element.11.gw), custom_call_target="tpu_custom_call" | custom-call | bytes 16777216 | tf_op jit(solution)/shard_map/pallas_call | solution.py:410

commit v4 on v3

--- a/solution.py
+++ b/solution.py
@@ -17,11 +17,14 @@
     W, H, T, SC, RC, SY, RY, XF, LG, STS, STR, TB, KLS, KLR, G, RT, GHS, GHR, GHK, ZS, ZR, GWS,
     ld, t_s, t_r, c_s, c_r, y_s, y_r, st_s, st_r, g_s, g_r, kl_s, kl_r, x_s, x_r, z_s, z_r, gw_s,
 ):
-    nv, nh, per, width = hid.shape
+    nz, nv = 2 * hid.shape[0], 4 * hid.shape[0]
+    nh, per, width = hid.shape[3:]
     vw = wgt.shape[1]
     half = per // 2
-    rows = nv * half
-    nz, ncb = nv // 2, GHS.shape[0] // 2
+    nq = H.shape[1]
+    nb = nv // 2
+    rows = nb * half
+    ncb = GHS.shape[0] // nq
     cw = width // ncb
     nt = vw // 4
     hv = vw // 2
@@ -36,19 +39,19 @@
             device_id={"vocab": v, "hid": h}, device_id_type=pl.DeviceIdType.MESH,
         )
 
-    def load_h(k, th):
+    def load_h(k, q):
         h = (h_far, h_y, h_core, me_h)[k]
         return pltpu.make_async_copy(
-            hid.at[:, h, pl.ds(th * half, half), :], H.at[h, th], ld.at[2 * k + th]
+            hid.at[:, q % 2, :, h, pl.ds(q // 2 * half, half), :], H.at[h, q], ld.at[nq * k + q]
         )
 
     def load_w(i):
         cols = pl.ds(pl.multiple_of(i * nt, nt), nt)
-        return pltpu.make_async_copy(wgt.at[:, cols], W.at[:, cols], ld.at[2 * nh + 2 + i])
+        return pltpu.make_async_copy(wgt.at[:, cols], W.at[:, cols], ld.at[nq * nh + 2 + i])
 
     for k in range(nh):
-        for th in range(2):
-            load_h(k, th).start()
+        for q in range(nq):
+            load_h(k, q).start()
         if k == 0:
             for i in range(vw // nt):
                 load_w(i).start()
@@ -57,7 +60,7 @@
         return teach.at[pl.ds(th * half, half), pl.ds(pl.multiple_of(v * vw, vw), vw)]
 
     own_t = [
-        pltpu.make_async_copy(teach_part(th, me_v), T.at[th, me_v], ld.at[2 * nh + th]) for th in range(2)
+        pltpu.make_async_copy(teach_part(th, me_v), T.at[2 * th + z % 2, z // 2 * 2 + x], ld.at[nq * nh + th]) for th in range(2)
     ]
     for copy in own_t:
         copy.start()
@@ -76,23 +79,23 @@
 
     def send_t(th, k):
         v = (me_v + k) % nv
-        return remote(teach_part(th, v), T.at[th, me_v], t_s.at[th, k], t_r.at[th, k], v, me_h)
+        return remote(teach_part(th, v), T.at[2 * th + z % 2, z // 2 * 2 + x], t_s.at[th, k], t_r.at[th, k], v, me_h)
 
     for k in range(1, nv):
         send_t(0, k).start()
 
     def project(k, out):
         h = (h_far, h_y, h_core, me_h)[k]
-        for th in range(2):
-            load_h(k, th).wait()
+        for q in range(nq):
+            load_h(k, q).wait()
 
         @pl.loop(0, vw // nt)
         def _(i):
             if k == 0:
                 load_w(i).wait()
             cols = pl.ds(pl.multiple_of(i * nt, nt), nt)
-            r = jnp.dot(H[h].reshape(2 * rows, width), W[:, cols], preferred_element_type=F32)
-            out[:, :, cols] = r.reshape(2, rows, nt)
+            r = jnp.dot(H[h].reshape(nq * rows, width), W[:, cols], preferred_element_type=F32)
+            out[:, :, cols] = r.reshape(nq, rows, nt)
 
     def core_copy(kind, th):
         return remote(
@@ -103,13 +106,13 @@
         return remote(SY.at[th], RY.at[th], y_s.at[th], y_r.at[th], me_v, h_y)
 
     project(0, SC.at[0])
-    for th in range(2):
+    for th in range(nq):
         core_copy(0, th).start()
     project(1, XF)
-    for th in range(2):
+    for th in range(nq):
         core_copy(0, th).wait_recv()
 
-        @pl.loop(0, nv)
+        @pl.loop(0, nb)
         def _(i):
             r16 = pl.ds(pl.multiple_of(i * half, half), half)
             s = XF[th, r16] + RC[0, th, r16]
@@ -119,17 +122,19 @@
             SY[th, r16, pl.ds(0, hv)] = hi * 4096.0 + lo
             SY[th, r16, pl.ds(hv, 128)] = jnp.broadcast_to(top, (half, 128))
 
-        if th == 0:
-            y_copy(0).start()
+        if th < 2:
+            y_copy(th).start()
     project(2, SC.at[1])
-    for th in range(2):
+    for th in range(nq):
         core_copy(1, th).start()
     project(3, LG)
     for k in range(1, nv):
         send_t(1, k).start()
 
-    lane = lax.broadcasted_iota(jnp.int32, (half, rows), 1)
+    lane = lax.broadcasted_iota(jnp.int32, (half, 128), 1)
+    live = lax.broadcasted_iota(jnp.int32, (1, 128), 1) < rows
     KLS[...] = jnp.zeros_like(KLS)
+    TB[...] = jnp.zeros_like(TB)
 
     def st_copy(th, k):
         return remote(
@@ -139,14 +144,15 @@
     def stats(th):
         core_copy(1, th).wait_recv()
         y_copy(th).wait_recv()
-        if th == 0:
-            y_copy(0).wait_send()
-            y_copy(1).start()
-        own_t[th].wait()
-        for k in range(1, nv):
-            send_t(th, k).wait_recv()
-
-        @pl.loop(0, nv)
+        y_copy(th).wait_send()
+        if th + 2 < nq:
+            y_copy(th + 2).start()
+        if th % 2 == 0:
+            own_t[th // 2].wait()
+            for k in range(1, nv):
+                send_t(th // 2, k).wait_recv()
+
+        @pl.loop(0, nb)
         def _(i):
             r16 = pl.ds(pl.multiple_of(i * half, half), half)
             f = RY[th, r16, pl.ds(0, hv)]
@@ -165,7 +171,7 @@
                 m, jnp.sum(e, axis=1, keepdims=True), jnp.sum(e * (l - t), axis=1, keepdims=True),
                 mt, jnp.sum(jnp.exp(t), axis=1, keepdims=True),
             ]
-            block = jnp.zeros((half, rows), F32)
+            block = jnp.zeros((half, 128), F32)
             for j, col in enumerate(cols):
                 block = jnp.where(lane == j, col, block)
             TB[r16, :] = block
@@ -196,14 +202,14 @@
             total_t = total_t + jnp.exp(m_t[d] - top_t) * s_t[d]
             total_a = total_a + w * (a[d] + s_s[d] * ((m_s[d] - top_s) - (m_t[d] - top_t)))
         log_s, log_t = jnp.log(total_s), jnp.log(total_t)
-        kl = total_a / total_s - log_s + log_t
+        kl = jnp.where(live, total_a / total_s - log_s + log_t, 0.0)
         KLS[th : th + 1, :] = kl
-        TB[0:1, :] = top_s + log_s
-        TB[1:2, :] = top_t + log_t
+        TB[0:1, :] = jnp.where(live, top_s + log_s, 0.0)
+        TB[1:2, :] = jnp.where(live, top_t + log_t, 0.0)
         TB[2:3, :] = kl
         TB[...] = TB[...].T
 
-        @pl.loop(0, nv)
+        @pl.loop(0, nb)
         def _(i):
             r16 = pl.ds(pl.multiple_of(i * half, half), half)
             b = TB[r16, :]
@@ -217,20 +223,23 @@
     def kl_copy(k):
         return remote(KLS, KLR.at[me_h], kl_s.at[k], kl_r.at[k], me_v, (me_h + k) % nh)
 
-    stats(0)
-    grad(0)
-    stats(1)
-    grad(1)
-    KLR[me_h] = KLS[...]
-    for k in range(1, nh):
-        kl_copy(k).start()
-
     def x_copy(s):
         return remote(GHS.at[s], GHR.at[s], x_s.at[s], x_r.at[s], 2 * z + 1 - x, me_h)
 
-    def z_copy(s, k):
-        to = (z + k) % nz
-        return remote(ZS.at[s, to], ZR.at[s, z], z_s.at[s, k], z_r.at[s, k], 2 * to + x, me_h)
+    def zp_of(s):
+        return s // ncb % 2
+
+    def z_copy(s, d, k):
+        return remote(
+            ZS.at[s, d], ZR.at[s, k], z_s.at[s, d], z_r.at[s, k], 2 * (zp_of(s) + 2 * d) + x, me_h
+        )
+
+    def z_sends(s, act):
+        for d in range(2):
+            for k in range(1, nz):
+                @pl.when((zp_of(s) + 2 * d + k) % nz == z)
+                def _():
+                    act(z_copy(s, d, k))
 
     def hidden_part(th):
         g_copy(th, 1).wait_recv()
@@ -245,25 +254,16 @@
                 G[:, th].reshape(nh * rows, vw), W[pl.ds(pl.multiple_of(cb * cw, cw), cw), :],
                 (((1,), (1,)), ((), ())), preferred_element_type=F32,
             )
-            RT[...] = r.reshape(nh, nz, 2, half, cw)
+            RT[...] = r.reshape(nh, 2, 2, half, cw)
             GHS[s] = RT[:, :, 1 - x].astype(BF16)
-            if th == 0:
-                @pl.when(cb < 2)
-                def _():
-                    x_copy(s).start()
+            x_copy(s).start()
             GHK[s] = RT[:, :, x]
 
     def pass_on(s):
         x_copy(s).wait()
-
-        @pl.when(s < 2 * ncb - 2)
-        def _():
-            x_copy(s + 2).start()
-
-        for to in range(nz):
-            ZS[s, to] = (GHK[s, :, to] + GHR[s, :, to].astype(F32)).astype(BF16)
-        for k in range(1, nz):
-            z_copy(s, k).start()
+        for d in range(2):
+            ZS[s, d] = (GHK[s, :, d] + GHR[s, :, d].astype(F32)).astype(BF16)
+        z_sends(s, lambda copy: copy.start())
 
     tile = width // 8
 
@@ -279,60 +279,73 @@
         def _():
             gw_copy(i - 2, slot).wait()
 
-        h = H[:, :, :, :, pl.ds(pl.multiple_of(i * tile, tile), tile)].reshape(2 * nh * rows, tile)
+        h = H[:, :, :, :, :, pl.ds(pl.multiple_of(i * tile, tile), tile)].reshape(nq * nh * rows, tile)
 
         @pl.loop(0, vw // nt)
         def _(j):
             cols = pl.ds(pl.multiple_of(j * nt, nt), nt)
             GWS[slot, :, cols] = lax.dot_general(
-                h, G[:, :, :, cols].reshape(2 * nh * rows, nt),
+                h, G[:, :, :, cols].reshape(nq * nh * rows, nt),
                 (((0,), (0,)), ((), ())), preferred_element_type=F32,
             ).astype(BF16)
 
         gw_copy(i, slot).start()
 
+    for q in range(3):
+        stats(q)
+        grad(q)
     hidden_part(0)
+    stats(3)
+    grad(3)
+    KLR[me_h] = KLS[...]
+    for k in range(1, nh):
+        kl_copy(k).start()
+    hidden_part(1)
     pass_on(0)
+    hidden_part(2)
     pass_on(1)
-    hidden_part(1)
+    pass_on(2)
+    hidden_part(3)
+    pass_on(3)
 
     @pl.loop(0, 8)
     def _(i):
         weight_tile(i)
 
-        @pl.when(i < 2 * ncb - 2)
+        @pl.when(i < 4)
         def _():
-            pass_on(i + 2)
+            pass_on(i + 4)
 
     for i in (6, 7):
         gw_copy(i, i % 2).wait()
-    for th in range(2):
-        @pl.loop(0, ncb)
-        def _(cb):
-            s = th * ncb + cb
-            total = ZS[s, z].astype(F32)
-            for k in range(1, nz):
-                z_copy(s, k).wait_recv()
-                total = total + ZR[s, (z + nz - k) % nz].astype(F32)
-            cols = pl.ds(pl.multiple_of(cb * cw, cw), cw)
-            gh_o[:, pl.ds(th * half, half), cols] = total.astype(BF16)
-            for k in range(1, nz):
-                z_copy(s, k).wait_send()
-
+    for q in range(nq):
+        @pl.when(z % 2 == q % 2)
+        def _():
+            for cb in range(ncb):
+                s = q * ncb + cb
+                total = ZS[s, z // 2].astype(F32)
+                for k in range(1, nz):
+                    pltpu.make_async_copy(ZR.at[s, k], ZR.at[s, k], z_r.at[s, k]).wait()
+                    total = total + ZR[s, k].astype(F32)
+                gh_o[:, pl.ds(q // 2 * half, half), pl.ds(cb * cw, cw)] = total.astype(BF16)
+
+    for s in range(nq * ncb):
+        z_sends(s, lambda copy: copy.wait_send())
     for k in range(1, nh):
         kl_copy(k).wait()
     kl_all = functools.reduce(jnp.add, [KLR[h] for h in range(nh)])
     kl_all = jnp.sum(jnp.sum(kl_all, axis=1, keepdims=True), axis=0, keepdims=True) / tokens
     loss_o[...] = kl_all
-    y_copy(1).wait_send()
-    for th in range(2):
+    for th in range(nq):
         for kind in range(2):
             core_copy(kind, th).wait_send()
         for which in range(3):
             g_copy(th, which).wait_send()
         for k in range(1, nv):
+            st_copy(th, k).wait_send()
+    for th in range(2):
+        for k in range(1, nv):
             send_t(th, k).wait_send()
-            st_copy(th, k).wait_send()
 
 
 def hand_out(loss, gh, gw, loss_o, gh_o, gw_o, buf, buf_h, sem_in, sem_out):
@@ -357,12 +370,13 @@
     tokens, width = student_hidden.shape
     vw = head_weight.shape[1]
     per = teacher_logits.shape[0]
-    half, nz, ncb = per // 2, nv // 2, 4
-    rows, cw, tile = nv * half, width // ncb, width // 8
-    hidden = student_hidden.reshape(nv, nh, per, width)
+    half, nz, nq, ncb = per // 2, nv // 2, 4, 2
+    nb = nv // 2
+    rows, cw, tile = nb * half, width // ncb, width // 8
+    hidden = student_hidden.reshape(nz // 2, 2, 2, nh, per, width)
     any_, vmem = pl.BlockSpec(memory_space=pl.ANY), pl.BlockSpec(memory_space=pltpu.VMEM)
     dma = lambda *shape: pltpu.SemaphoreType.DMA(shape)
-    steps = 2 * ncb
+    steps = nq * ncb
     loss, gh, gw = pl.pallas_call(
         functools.partial(fused, tokens),
         out_shape=(
@@ -374,30 +388,30 @@
         out_specs=(vmem, vmem, any_),
         scratch_shapes=[
             pltpu.VMEM((width, vw), BF16),
-            pltpu.VMEM((nh, 2, nv, half, width), BF16),
-            pltpu.VMEM((2, nv, half, vw), BF16),
-            pltpu.VMEM((2, 2, rows, vw), F32),
-            pltpu.VMEM((2, 2, rows, vw), F32),
-            pltpu.VMEM((2, rows, vw // 2 + 128), F32),
-            pltpu.VMEM((2, rows, vw // 2 + 128), F32),
-            pltpu.VMEM((2, rows, vw), F32),
-            pltpu.VMEM((2, rows, vw), F32),
-            pltpu.VMEM((2, 8, rows), F32),
-            pltpu.VMEM((2, nv, 8, rows), F32),
-            pltpu.VMEM((rows, rows), F32),
-            pltpu.VMEM((8, rows), F32),
-            pltpu.VMEM((nh, 8, rows), F32),
-            pltpu.VMEM((nh, 2, rows, vw), BF16),
-            pltpu.VMEM((nh, nz, 2, half, cw), F32),
-            pltpu.VMEM((steps, nh, nz, half, cw), BF16),
-            pltpu.VMEM((steps, nh, nz, half, cw), BF16),
-            pltpu.VMEM((steps, nh, nz, half, cw), F32),
-            pltpu.VMEM((steps, nz, nh, half, cw), BF16),
+            pltpu.VMEM((nh, nq, 2, 2, half, width), BF16),
+            pltpu.VMEM((nq, nb, half, vw), BF16),
+            pltpu.VMEM((2, nq, rows, vw), F32),
+            pltpu.VMEM((2, nq, rows, vw), F32),
+            pltpu.VMEM((nq, rows, vw // 2 + 128), F32),
+            pltpu.VMEM((nq, rows, vw // 2 + 128), F32),
+            pltpu.VMEM((nq, rows, vw), F32),
+            pltpu.VMEM((nq, rows, vw), F32),
+            pltpu.VMEM((nq, 8, 128), F32),
+            pltpu.VMEM((nq, nv, 8, 128), F32),
+            pltpu.VMEM((128, 128), F32),
+            pltpu.VMEM((8, 128), F32),
+            pltpu.VMEM((nh, 8, 128), F32),
+            pltpu.VMEM((nh, nq, rows, vw), BF16),
+            pltpu.VMEM((nh, 2, 2, half, cw), F32),
+            pltpu.VMEM((steps, nh, 2, half, cw), BF16),
+            pltpu.VMEM((steps, nh, 2, half, cw), BF16),
+            pltpu.VMEM((steps, nh, 2, half, cw), F32),
+            pltpu.VMEM((steps, 2, nh, half, cw), BF16),
             pltpu.VMEM((steps, nz, nh, half, cw), BF16),
             pltpu.VMEM((2, tile, vw), BF16),
-            dma(2 * nh + 2 + 4),
-            dma(2, nv), dma(2, nv), dma(2, 2), dma(2, 2), dma(2), dma(2), dma(2, nv), dma(2, nv),
-            dma(2, 3), dma(2, 3), dma(nh), dma(nh), dma(steps), dma(steps), dma(steps, nz), dma(steps, nz),
+            dma(nq * nh + 2 + 4),
+            dma(2, nv), dma(2, nv), dma(2, nq), dma(2, nq), dma(nq), dma(nq), dma(nq, nv), dma(nq, nv),
+            dma(nq, 3), dma(nq, 3), dma(nh), dma(nh), dma(steps), dma(steps), dma(steps, 2), dma(steps, nz),
             dma(2),
         ],
         compiler_params=pltpu.CompilerParams(

time: 123 us -> 122 us (level); the launches traced: 121 us -> 122 us
  no operation moved by 1% of the time
where the time goes in v4:
time: 122 us
  Pallas kernels  121 us (99%)
    pallas_call x1, Pallas kernels, fused_shards(): pl.pallas_call(functools.partial(fused, tokens), out_shape=(jax.ShapeDtyp...  114 us
    pallas_call x1, Pallas kernels, fused_shards(): pl.pallas_call(hand_out, out_shape=tuple((jax.ShapeDtypeStruct(a.shape, a...  7.69 us

profile of v4, /device:TPU:8, one launch (start us, length us, event | category | flops | bytes accessed | tf_op | source)
XLA Modules:
  0.0 121.9 jit_solution(18396196731975823334)
XLA Ops:
  0.6 113.5 %shard_map.58 = (f32[1,1]{1,0:T(1,128)}, bf16[4,32,2048]{2,1,0:T(8,128)(2,1)}, bf16[2048,2048]{1,0:T(8,128)(2,1)}) custom-call(bf16[2,2,2,4,32,2048]{5,4,3,2,1,0:T(8,128)(2,1)} %bitcast.3, bf16[2048,2048]{1,0:T(8,128)(2,1)} %wgt.1, bf16[32,16384]{1,0:T(8,128)(2,1)} %teach.1), custom_call_target="tpu_custom_call" | custom-call | flops 25769803776 | bytes 16777216 | tf_op jit(solution)/shard_map/pallas_call | solution.py:380
  114.2 7.7 %shard_map.59 = (f32[1,1]{1,0:T(1,128)}, bf16[4,32,2048]{2,1,0:T(8,128)(2,1)}, bf16[2048,2048]{1,0:T(8,128)(2,1)}) custom-call(f32[1,1]{1,0:T(1,128)} %get-tuple-element.9.loss, bf16[4,32,2048]{2,1,0:T(8,128)(2,1)} %get-tuple-element.10.gh, bf16[2048,2048]{1,0:T(8,128)(2,1)} %get-tuple-element.11.gw), custom_call_target="tpu_custom_call" | custom-call | bytes 16777216 | tf_op jit(solution)/shard_map/pallas_call | solution.py:424

commit v5 on v4

--- a/solution.py
+++ b/solution.py
@@ -14,7 +14,7 @@
 
 def fused(
     tokens, hid, wgt, teach, loss_o, gh_o, gw_o,
-    W, H, T, SC, RC, SY, RY, XF, LG, STS, STR, TB, KLS, KLR, G, RT, GHS, GHR, GHK, ZS, ZR, GWS,
+    W, H, T, SC, RC, SY, RY, XF, LG, STS, STR, TB, KLS, KLR, G, RT, GHS, GHR, GHK, ZS, ZR, GWS, HT,
     ld, t_s, t_r, c_s, c_r, y_s, y_r, st_s, st_r, g_s, g_r, kl_s, kl_r, x_s, x_r, z_s, z_r, gw_s,
 ):
     nz, nv = 2 * hid.shape[0], 4 * hid.shape[0]
@@ -124,12 +124,31 @@
 
         if th < 2:
             y_copy(th).start()
-    project(2, SC.at[1])
+    for k in (2, 3):
+        for q in range(nq):
+            load_h(k, q).wait()
+
+    @pl.loop(0, vw // nt)
+    def _(i):
+        cols = pl.ds(pl.multiple_of(i * nt, nt), nt)
+        r = jnp.dot(
+            H[pl.ds(2 * y, 2)].reshape(2 * nq * rows, width), W[:, cols], preferred_element_type=F32
+        )
+        r = r.reshape(2, nq, rows, nt)
+        first = c == 0
+        SC[1, :, :, cols] = jnp.where(first, r[1], r[0])
+        LG[:, :, cols] = jnp.where(first, r[0], r[1])
+
     for th in range(nq):
         core_copy(1, th).start()
-    project(3, LG)
     for k in range(1, nv):
         send_t(1, k).start()
+
+    @pl.loop(0, width // 256)
+    def _(i):
+        d = pl.ds(pl.multiple_of(i * 256, 256), 256)
+        HT[d, :] = H[:, :, :, :, :, d].reshape(nh * nq * rows, 256).T
+
 
     lane = lax.broadcasted_iota(jnp.int32, (half, 128), 1)
     live = lax.broadcasted_iota(jnp.int32, (1, 128), 1) < rows
@@ -265,7 +284,7 @@
             ZS[s, d] = (GHK[s, :, d] + GHR[s, :, d].astype(F32)).astype(BF16)
         z_sends(s, lambda copy: copy.start())
 
-    tile = width // 8
+    tile = width // 4
 
     def gw_copy(i, slot):
         return pltpu.make_async_copy(
@@ -279,14 +298,14 @@
         def _():
             gw_copy(i - 2, slot).wait()
 
-        h = H[:, :, :, :, :, pl.ds(pl.multiple_of(i * tile, tile), tile)].reshape(nq * nh * rows, tile)
+        h = pl.ds(pl.multiple_of(i * tile, tile), tile)
 
         @pl.loop(0, vw // nt)
         def _(j):
             cols = pl.ds(pl.multiple_of(j * nt, nt), nt)
             GWS[slot, :, cols] = lax.dot_general(
-                h, G[:, :, :, cols].reshape(nq * nh * rows, nt),
-                (((0,), (0,)), ((), ())), preferred_element_type=F32,
+                HT[h, :], G[:, :, :, cols].reshape(nq * nh * rows, nt),
+                (((1,), (0,)), ((), ())), preferred_element_type=F32,
             ).astype(BF16)
 
         gw_copy(i, slot).start()
@@ -308,15 +327,12 @@
     hidden_part(3)
     pass_on(3)
 
-    @pl.loop(0, 8)
+    @pl.loop(0, 4)
     def _(i):
         weight_tile(i)
-
-        @pl.when(i < 4)
-        def _():
-            pass_on(i + 4)
-
-    for i in (6, 7):
+        pass_on(i + 4)
+
+    for i in (2, 3):
         gw_copy(i, i % 2).wait()
     for q in range(nq):
         @pl.when(z % 2 == q % 2)
@@ -372,7 +388,7 @@
     per = teacher_logits.shape[0]
     half, nz, nq, ncb = per // 2, nv // 2, 4, 2
     nb = nv // 2
-    rows, cw, tile = nb * half, width // ncb, width // 8
+    rows, cw, tile = nb * half, width // ncb, width // 4
     hidden = student_hidden.reshape(nz // 2, 2, 2, nh, per, width)
     any_, vmem = pl.BlockSpec(memory_space=pl.ANY), pl.BlockSpec(memory_space=pltpu.VMEM)
     dma = lambda *shape: pltpu.SemaphoreType.DMA(shape)
@@ -409,6 +425,7 @@
             pltpu.VMEM((steps, 2, nh, half, cw), BF16),
             pltpu.VMEM((steps, nz, nh, half, cw), BF16),
             pltpu.VMEM((2, tile, vw), BF16),
+            pltpu.VMEM((width, nh * nq * rows), BF16),
             dma(nq * nh + 2 + 4),
             dma(2, nv), dma(2, nv), dma(2, nq), dma(2, nq), dma(nq), dma(nq), dma(nq, nv), dma(nq, nv),
             dma(nq, 3), dma(nq, 3), dma(nh), dma(nh), dma(steps), dma(steps), dma(steps, 2), dma(steps, nz),

time: 122 us -> 121 us (level)
  no operation moved by 1% of the time
where the time goes in v5:
time: 121 us
  Pallas kernels  121 us (100%)
    pallas_call x1, Pallas kernels, fused_shards(): pl.pallas_call(functools.partial(fused, tokens), out_shape=(jax.ShapeDtyp...  113 us
    pallas_call x1, Pallas kernels, fused_shards(): pl.pallas_call(hand_out, out_shape=tuple((jax.ShapeDtypeStruct(a.shape, a...  7.69 us

profile of v5, /device:TPU:8, one launch (start us, length us, event | category | flops | bytes accessed | tf_op | source)
XLA Modules:
  0.0 121.2 jit_solution(451723865836533490)
XLA Ops:
  0.6 112.9 %shard_map.58 = (f32[1,1]{1,0:T(1,128)}, bf16[4,32,2048]{2,1,0:T(8,128)(2,1)}, bf16[2048,2048]{1,0:T(8,128)(2,1)}) custom-call(bf16[2,2,2,4,32,2048]{5,4,3,2,1,0:T(8,128)(2,1)} %bitcast.3, bf16[2048,2048]{1,0:T(8,128)(2,1)} %wgt.1, bf16[32,16384]{1,0:T(8,128)(2,1)} %teach.1), custom_call_target="tpu_custom_call" | custom-call | flops 25769803776 | bytes 16777216 | tf_op jit(solution)/shard_map/pallas_call | solution.py:396
  113.5 7.7 %shard_map.59 = (f32[1,1]{1,0:T(1,128)}, bf16[4,32,2048]{2,1,0:T(8,128)(2,1)}, bf16[2048,2048]{1,0:T(8,128)(2,1)}) custom-call(f32[1,1]{1,0:T(1,128)} %get-tuple-element.9.loss, bf16[4,32,2048]{2,1,0:T(8,128)(2,1)} %get-tuple-element.10.gh, bf16[2048,2048]{1,0:T(8,128)(2,1)} %get-tuple-element.11.gw), custom_call_target="tpu_custom_call" | custom-call | bytes 16777216 | tf_op jit(solution)/shard_map/pallas_call | solution.py:441
